TPU v7x, 32 devices: a whole 2x2x4 slice. The times are simulated.
32 devices in a mesh: groups: 2 (over y), expert: 4 (over z), tensor: 2 (over x), dp: 2 (over core).
Axes of the slice: x: 2, y: 2, z: 4, core: 2. Of those that a mesh axis runs over, the one named last changes fastest.
Arguments:
- attn: bfloat16 [1024, 4096], P(('groups', 'expert', 'dp'), 'tensor'), parts along dimension 0, may hold values from -6 to 6
- o_weight: bfloat16 [4096, 4096], P('tensor', 'dp'), may hold values from -0.09375 to 0.09375
- residual: bfloat16 [1024, 4096], P(('groups', 'expert', 'dp'), 'tensor'), parts along dimension 0, may hold values from -100 to 100
- norm_gain: bfloat16 [4096], replicated, may hold values from 0.099609375 to 1.8984375
- expert_ids: int32 [1024, 8], P(('groups', 'expert', 'dp')), parts along dimension 0, may hold values from 0 to 31, all different within a row; in each aligned block of 64 rows (0 to 63, 64 to 127, ...) at most 24 rows name the same one
- route_weights: float32 [1024, 8], P(('groups', 'expert', 'dp')), parts along dimension 0, may hold values from 0.1 to 1
- w_gate: bfloat16 [32, 4096, 1024], P(('expert', 'dp'), None, 'tensor'), may hold values from -0.09375 to 0.09375
- w_up: bfloat16 [32, 4096, 1024], P(('expert', 'dp'), None, 'tensor'), may hold values from -0.09375 to 0.09375
- w_down: bfloat16 [32, 1024, 4096], P(('expert', 'dp'), 'tensor'), may hold values from -0.25 to 0.25
Outputs:
- moe_out: bfloat16 [1024, 4096], P(('groups', 'expert', 'dp'), 'tensor'), parts along dimension 0
There are 2 independent parts, one for each index of `groups`. A program takes and returns all parts, laid end to end along the dimension named above; an argument that names none is the same for every part. Nothing has to cross between parts.
Inputs may be any that keep to these rules, and one draw needn't show every extreme that they name: `expert_ids`: each row names 8 different experts. Within each aligned block of 64 rows (the rows of one device) no expert is named by more than 24 rows, and in every draw some block has an expert named by exactly 24 rows.
All inputs are finite; a program needn't handle non-finite values.
Results may differ from a plain program's by a relative error of at most 0.024.
Values may be sent and summed in bfloat16 or wider, within the bound.
A program may use at most 128 MiB of HBM per device.

v0:
```python
import jax
import jax.numpy as jnp
from jax import lax
from jax.sharding import PartitionSpec as P

EXPERTS = 32
SLOT = 24


epsilon = 1e-06


def on_device(attn, o_weight, residual, norm_gain, expert_ids, route_weights, w_gate, w_up, w_down):
    rows_here = attn.shape[0]
    width = norm_gain.shape[0]
    pieces = lax.axis_size("tensor")
    quarter = width // pieces
    offset = lax.axis_index("tensor") * quarter
    partial_value = jnp.dot(
        attn, lax.all_gather(o_weight, "dp", axis=1, tiled=True), preferred_element_type=jnp.float32
    )
    own_cols = lax.dynamic_slice_in_dim(partial_value, offset, quarter, 1) + residual.astype(
        jnp.float32
    )
    partial_value = lax.dynamic_update_slice_in_dim(partial_value, own_cols, offset, 1)
    summed = lax.psum(partial_value.astype(jnp.bfloat16), "tensor")
    rounded = lax.optimization_barrier(summed)
    hidden_f = rounded.astype(jnp.float32)
    inverse = lax.rsqrt(jnp.mean(hidden_f * hidden_f, axis=1) + epsilon)
    payload = (hidden_f * inverse[:, None] * norm_gain.astype(jnp.float32)[None, :]).astype(
        jnp.bfloat16
    )
    onehot = (expert_ids[:, :, None] == jnp.arange(EXPERTS, dtype=jnp.int32)).astype(jnp.float32)
    chosen = jnp.sum(onehot, axis=1)
    row_ids = jnp.arange(rows_here)
    earlier = (row_ids[:, None] > row_ids[None, :]).astype(jnp.float32)
    before = jnp.dot(earlier, chosen, precision=lax.Precision.HIGHEST)
    slot_ids = jnp.arange(SLOT, dtype=jnp.float32)
    placing = (
        (before.T[:, None, :] == slot_ids[None, :, None]) & (chosen.T[:, None, :] > 0.5)
    ).astype(jnp.float32)
    outgoing = jnp.einsum(
        "ecr,rd->ecd", placing.astype(jnp.bfloat16), payload, preferred_element_type=jnp.float32
    ).astype(jnp.bfloat16)
    sources = lax.axis_size(("expert", "dp"))
    held_experts = w_gate.shape[0]
    outgoing = outgoing.reshape(sources, held_experts, SLOT, payload.shape[1])
    arrived_rows = lax.all_to_all(
        outgoing, ("expert", "dp"), split_axis=0, concat_axis=0, tiled=True
    )
    gate_acc = jnp.einsum(
        "sjcd,jdf->sjcf", arrived_rows, w_gate, preferred_element_type=jnp.float32
    )
    up_acc = jnp.einsum("sjcd,jdf->sjcf", arrived_rows, w_up, preferred_element_type=jnp.float32)
    activated = (jax.nn.silu(gate_acc) * up_acc).astype(jnp.bfloat16)
    partials = jnp.einsum("sjcf,jfd->sjcd", activated, w_down, preferred_element_type=jnp.float32)
    outputs = lax.psum_scatter(
        partials.astype(jnp.bfloat16), "tensor", scatter_dimension=3, tiled=True
    )
    returned = lax.all_to_all(outputs, ("expert", "dp"), split_axis=0, concat_axis=0, tiled=True)
    returned = returned.reshape(EXPERTS, SLOT, quarter).astype(jnp.float32)
    weight_map = jnp.sum(route_weights[:, :, None] * onehot, axis=1)
    weighted = placing * weight_map.T[:, None, :]
    moe_out = jnp.einsum(
        "ecr,ecd->rd",
        weighted,
        returned,
        precision=lax.Precision.HIGHEST,
        preferred_element_type=jnp.float32,
    )
    return moe_out.astype(jnp.bfloat16)


def solution(mesh):
    placed = (
        P(("groups", "expert", "dp"), "tensor"),
        P("tensor", "dp"),
        P(("groups", "expert", "dp"), "tensor"),
        P(),
        P(("groups", "expert", "dp"), None),
        P(("groups", "expert", "dp"), None),
        P(("expert", "dp"), None, "tensor"),
        P(("expert", "dp"), None, "tensor"),
        P(("expert", "dp"), "tensor", None),
    )
    return jax.shard_map(
        on_device,
        mesh=mesh,
        in_specs=placed,
        out_specs=P(("groups", "expert", "dp"), "tensor"),
        check_vma=False,
    )
```

profile of v0, /device:TPU:0, one launch (start us, length us, event | category | flops | bytes accessed | tf_op | source)
XLA Modules:
  0.0 422.1 jit_solution(4321058223457081654)
XLA Ops:
  6.5 0.7 all-gather.2.cloned.1.call-update
  7.3 0.0 all-reduce.2.cloned.1.call-start
  7.4 0.0 copy-start.2
  7.4 0.0 copy-start.3
  7.4 34.3 %all-gather.2.cloned.1.call-done = bf16[2048,4096]{1,0:T(8,128)(2,1)} async-done(((bf16[2048,2048]{1,0:T(8,128)(2,1)}), bf16[2048,4096]{1,0:T(8,128)(2,1)}) %all-gather.2.cloned.1.call-update) | async-done | bytes 16777232 | tf_op jit(solution)/shard_map/all_gather | solution.py:20
  41.7 8.8 %fusion.47 = f32[64,4096]{1,0:T(8,128)S(1)} fusion(bf16[64,2048]{1,0:T(8,128)(2,1)S(1)} %copy-done, bf16[2048,4096]{1,0:T(8,128)(2,1)} %all-gather.2.cloned.1.call-done), kind=kOutput, calls=%fused_computation.48 | convolution fusion | flops 1073741824 | bytes 18087936 | tf_op jit(solution)/shard_map/dot_general | solution.py:19
  50.5 0.1 add_dynamic-update-slice_fusion
  50.6 0.8 convert_element_type.45
  51.5 0.0 all-reduce.2.cloned.1.call-update
  51.5 0.0 reduce-scatter.2.cloned.1.call-start
  51.6 0.1 fusion.45
  51.7 0.1 convert_convert_fusion
  51.8 29.6 %all-reduce.2.cloned.1.call-done = bf16[64,4096]{1,0:T(8,128)(2,1)} async-done(((bf16[64,4096]{1,0:T(8,128)(2,1)}), bf16[64,4096]{1,0:T(8,128)(2,1)}) %all-reduce.2.cloned.1.call-update) | async-done | bytes 524304 | tf_op jit(solution)/shard_map/psum | solution.py:26
  81.4 1.2 fusion.30
  82.7 2.9 convolution_convert_fusion
  85.7 143.5 %all_to_all.10 = bf16[8,4,24,4096]{3,2,1,0:T(8,128)(2,1)S(1)} all-to-all(bf16[8,4,24,4096]{3,2,1,0:T(8,128)(2,1)S(1)} %bitcast.56), channel_id=1, replica_groups=mesh['groups'=2,'expert'=4,'tensor'=2,'dp'=2] {'expert','dp'}, dimensions={0} | all-to-all | bytes 12582912 | tf_op jit(solution)/shard_map/all_to_all | solution.py:48
  229.2 7.7 %fusion.4 = f32[4,8,24,512]{3,2,1,0:T(8,128)S(1)} fusion(bf16[4,4096,512]{2,1,0:T(8,128)(2,1)} %param.15, bf16[8,4,24,4096]{3,2,1,0:T(8,128)(2,1)S(1)} %all_to_all.10), kind=kOutput, calls=%fused_computation.4 | convolution fusion | flops 3221225472 | bytes 24641536 | tf_op jit(solution)/shard_map/sjcd,jdf->sjcf/dot_general | solution.py:51
  236.9 9.6 %fusion.22 = bf16[8,4,24,512]{3,2,0,1:T(8,128)(2,1)S(1)} fusion(f32[4,8,24,512]{3,2,1,0:T(8,128)S(1)} %fusion.4, bf16[4,4096,512]{2,1,0:T(8,128)(2,1)} %param.16, bf16[8,4,24,4096]{3,2,1,0:T(8,128)(2,1)S(1)} %all_to_all.10), kind=kOutput, calls=%fused_computation.16 | convolution fusion | flops 3223584768 | bytes 25427968 | tf_op jit(solution)/shard_map/sjcd,jdf->sjcf/dot_general | solution.py:54
  246.5 11.9 %fusion.9 = bf16[8,4,24,4096]{3,2,0,1:T(8,128)(2,1)} fusion(bf16[8,4,24,512]{3,2,0,1:T(8,128)(2,1)S(1)} %fusion.22, bf16[4,512,4096]{2,1,0:T(8,128)(2,1)} %param.17), kind=kOutput, calls=%fused_computation.8 | convolution fusion | flops 3224371200 | bytes 23855104 | tf_op jit(solution)/shard_map/sjcf,jfd->sjcd/dot_general | solution.py:56
  258.4 0.0 reduce-scatter.2.cloned.1.call-update
  258.4 75.0 %reduce-scatter.2.cloned.1.call-done = bf16[8,4,24,2048]{3,2,0,1:T(8,128)(2,1)} async-done(((bf16[8,4,24,4096]{3,2,0,1:T(8,128)(2,1)}), bf16[8,4,24,2048]{3,2,0,1:T(8,128)(2,1)}) %reduce-scatter.2.cloned.1.call-update) | async-done | bytes 3145744 | tf_op jit(solution)/shard_map/reduce_scatter | solution.py:57
  333.4 2.3 copy.30
  335.7 75.9 %all_to_all.11 = bf16[8,4,24,2048]{3,2,1,0:T(8,128)(2,1)S(1)} all-to-all(bf16[8,4,24,2048]{3,2,1,0:T(8,128)(2,1)S(1)} %copy.30), channel_id=1, replica_groups=mesh['groups'=2,'expert'=4,'tensor'=2,'dp'=2] {'expert','dp'}, dimensions={0} | all-to-all | bytes 6291456 | tf_op jit(solution)/shard_map/all_to_all | solution.py:60
  411.7 3.9 fusion.19
  (15 shorter events, 0.1 us)
Async XLA Ops:
  6.5 35.2 %copy-start = (bf16[64,2048]{1,0:T(8,128)(2,1)S(1)}, bf16[64,2048]{1,0:T(8,128)(2,1)}, u32[]{:S(2)}) copy-start(bf16[64,2048]{1,0:T(8,128)(2,1)} %param.9) | copy-start | bytes 786436
  6.5 0.8 copy-start.4
  6.5 0.8 copy-start.5
  6.5 35.2 %all-gather.2.cloned.1.call-start = ((), (), s32[]{:S(2)}) async-start(), calls=%async_computation.3 | async-start | bytes 25165824 | tf_op jit(solution)/shard_map/all_gather | solution.py:20
  7.3 74.2 %all-reduce.2.cloned.1.call-start = ((), (), s32[]{:S(2)}) async-start(), calls=%async_computation.4 | async-start | bytes 1048576 | tf_op jit(solution)/shard_map/psum | solution.py:26
  7.4 43.1 %copy-start.2 = (bf16[64,2048]{1,0:T(8,128)(2,1)S(1)}, bf16[64,2048]{1,0:T(8,128)(2,1)}, u32[]{:S(2)}) copy-start(bf16[64,2048]{1,0:T(8,128)(2,1)} %param.11) | copy-start | bytes 786436
  7.4 44.2 %copy-start.3 = (bf16[4096]{0:T(1024)(128)(2,1)S(1)}, bf16[4096]{0:T(1024)(128)(2,1)}, u32[]{:S(2)}) copy-start(bf16[4096]{0:T(1024)(128)(2,1)} %param.12) | copy-start | bytes 24580
  51.5 281.9 %reduce-scatter.2.cloned.1.call-start = ((), (), s32[]{:S(2)}) async-start(), calls=%async_computation.5 | async-start | bytes 9437184 | tf_op jit(solution)/shard_map/reduce_scatter | solution.py:57
  333.4 82.2 %copy-start.1 = (bf16[64,2048]{1,0:T(8,128)(2,1)S(1)}, bf16[64,2048]{1,0:T(8,128)(2,1)}, u32[]{:S(2)}) copy-start(bf16[64,2048]{1,0:T(8,128)(2,1)} %param.9) | copy-start | bytes 786436
Sparse Core Ops, SparseCore 0:
  8.9 32.7 all-gather.1
  51.6 29.7 all-reduce.1
  258.5 74.8 reduce-scatter.1
where the time goes:
time: 422 us
  blocking collectives  219 us (52%)
  waiting for transfers between devices  140 us (33%)
  matrix products  44.9 us (11%)
  between operations  13.2 us (3%)
    all_to_all x1, blocking collectives, on_device(): lax.all_to_all(outgoing, ('expert', 'dp'), split_axis=0, concat_axis=0, t...  144 us
    all_to_all x1, blocking collectives, on_device(): lax.all_to_all(outputs, ('expert', 'dp'), split_axis=0, concat_axis=0, ti...  75.9 us
    reduce_scatter x1, waiting for transfers between devices, on_device(): lax.psum_scatter(partials.astype(jnp.bfloat16), 'tensor', scatter_dimensi...  75 us
    all_gather x1, waiting for transfers between devices, on_device(): lax.all_gather(o_weight, 'dp', axis=1, tiled=True)  34.3 us
    psum x1, waiting for transfers between devices, on_device(): summed = lax.psum(partial_value.astype(jnp.bfloat16), 'tensor')  29.6 us
    dot_general x1, matrix products, on_device(): jnp.einsum('sjcf,jfd->sjcd', activated, w_down, preferred_element_type=jn...  11.9 us
    dot_general x1, matrix products, on_device(): jnp.einsum('sjcd,jdf->sjcf', arrived_rows, w_up, preferred_element_type=j...  9.58 us
    dot_general x1, matrix products, on_device(): jnp.dot(attn, lax.all_gather(o_weight, 'dp', axis=1, tiled=True), preferr...  8.78 us
  transfers between devices with their start and end apart: 3, of which 3 were waited for; matrix products, arithmetic and copies ran while one was open for 0% of the time, Pallas kernels for 0%

commit v1 on v0

v1 whole, which is shorter than its diff:
```python
import functools

import jax
import jax.numpy as jnp
from jax import lax
from jax.experimental import pallas as pl
from jax.experimental.pallas import tpu as pltpu
from jax.sharding import PartitionSpec as P

MESH = pl.DeviceIdType.MESH
epsilon = 1e-06
MIB = 1 << 20


def greet(z, t, d, n_z, n_t, n_d, square):
    barrier = pltpu.get_barrier_semaphore()
    count = 0
    for i in range(n_t):
        for j in range(n_d):
            if (i or j) and (square or not (i and j)):
                pl.semaphore_signal(
                    barrier,
                    inc=1,
                    device_id={"tensor": lax.rem(t + i, n_t), "dp": lax.rem(d + j, n_d)},
                    device_id_type=MESH,
                )
                count += 1
    for i in range(1, n_z):
        pl.semaphore_signal(
            barrier, inc=1, device_id={"expert": lax.rem(z + i, n_z)}, device_id_type=MESH
        )
        count += 1
    pl.semaphore_wait(barrier, count)


def gather_kernel(
    n_z, n_t, n_d, attn, ow_hbm, residual, gain, out,
    pair, ow, part, landed, squares,
    ow_sem, a_send, a_recv, p_send, p_recv, s_send, s_recv,
    z_send, z_recv, x_send, x_recv, c_send, c_recv,
):
    z, t, d = lax.axis_index("expert"), lax.axis_index("tensor"), lax.axis_index("dp")
    rows, depth = attn.shape
    width = residual.shape[1]
    held = ow.shape[1]
    blocks = held // width
    load = pltpu.make_async_copy(ow_hbm, ow, ow_sem)
    load.start()
    greet(z, t, d, n_z, n_t, n_d, True)

    pair[pl.ds(d * rows, rows), :] = attn[...]
    sent = []
    for j in range(1, n_d):
        copy = pltpu.make_async_remote_copy(
            attn, pair.at[pl.ds(d * rows, rows), :], a_send.at[j], a_recv.at[j],
            device_id={"dp": lax.rem(d + j, n_d)}, device_id_type=MESH,
        )
        copy.start()
        sent.append(copy)
    load.wait()
    for copy in sent:
        copy.wait()

    tile = min(512, width)
    for first in range(0, held, tile):
        part[:, pl.ds(first, tile)] = jnp.dot(
            pair[...], ow[:, pl.ds(first, tile)], preferred_element_type=jnp.float32
        ).astype(jnp.bfloat16)

    def piece(i, j):
        owner, core = d * blocks + i, lax.rem(d + j, n_d)
        source = part.at[pl.ds(core * rows, rows), pl.ds(i * width, width)]
        copy = pltpu.make_async_remote_copy(
            source, landed.at[t], p_send.at[i, j], p_recv.at[t],
            device_id={"tensor": owner, "dp": core}, device_id_type=MESH,
        )
        return owner, core, copy

    for i in range(blocks):
        for j in range(n_d):
            owner, core, copy = piece(i, j)
            if j:
                copy.start()
            else:
                @pl.when(owner != t)
                def _():
                    copy.start()

                @pl.when(owner == t)
                def _():
                    landed[t] = part[pl.ds(d * rows, rows), pl.ds(i * width, width)]

    for i in range(n_t):
        arrival = pltpu.make_async_remote_copy(
            landed.at[i], landed.at[i], p_send.at[0, 0], p_recv.at[i],
            device_id={"tensor": i}, device_id_type=MESH,
        )

        @pl.when(jnp.logical_or(i != t, t // blocks != d))
        def _():
            arrival.wait_recv()

    hidden = residual[...].astype(jnp.float32)
    for i in range(n_t):
        hidden = hidden + landed[i].astype(jnp.float32)
    hidden = hidden.astype(jnp.bfloat16).astype(jnp.float32)
    squares[0] = jnp.broadcast_to(
        jnp.sum(hidden * hidden, axis=1, keepdims=True), squares.shape[1:]
    )
    sums = []
    for i in range(1, n_t):
        copy = pltpu.make_async_remote_copy(
            squares.at[0], squares.at[i], s_send.at[i], s_recv.at[i],
            device_id={"tensor": lax.rem(t + i, n_t)}, device_id_type=MESH,
        )
        copy.start()
        sums.append(copy)
    for copy in sums:
        copy.wait()
    total = squares[0]
    for i in range(1, n_t):
        total = total + squares[i]
    inverse = lax.rsqrt(total[:, :1] / (width * n_t) + epsilon)
    columns = pl.ds(pl.multiple_of(t * width, width), width)
    normed = hidden * inverse * gain[:, columns].astype(jnp.float32)

    def block(core, chip, half):
        return out.at[
            pl.ds(pl.multiple_of((core * n_z + chip) * rows, rows), rows),
            pl.ds(pl.multiple_of(half * width, width), width),
        ]

    block(d, z, t)[...] = normed.astype(jnp.bfloat16)

    started = []

    def to_tensor(i, chip):
        copies = []
        for h in range(1, n_t):
            ref = block(d, lax.rem(z - chip + n_z, n_z), t)
            copy = pltpu.make_async_remote_copy(
                ref, ref, x_send.at[h, chip], x_recv.at[h, chip],
                device_id={"tensor": lax.rem(t + h, n_t)}, device_id_type=MESH,
            )
            copy.start()
            copies.append(copy)
        started.extend(copies)

    def to_core(h, chip):
        for j in range(1, n_d):
            ref = block(d, lax.rem(z - chip + n_z, n_z), lax.rem(t - h + n_t, n_t))
            copy = pltpu.make_async_remote_copy(
                ref, ref, c_send.at[j, h, chip], c_recv.at[j, h, chip],
                device_id={"dp": lax.rem(d + j, n_d)}, device_id_type=MESH,
            )
            copy.start()
            started.append(copy)

    to_tensor(t, 0)
    order = sorted(range(1, n_z), key=lambda i: min(i, n_z - i))
    for i in order:
        ref = block(d, z, t)
        copy = pltpu.make_async_remote_copy(
            ref, ref, z_send.at[i], z_recv.at[i],
            device_id={"expert": lax.rem(z + i, n_z)}, device_id_type=MESH,
        )
        copy.start()
        started.append(copy)
    to_core(0, 0)

    def await_block(ref, sem):
        pltpu.make_async_remote_copy(
            ref, ref, z_send.at[0], sem, device_id={"tensor": t}, device_id_type=MESH
        ).wait_recv()

    def from_tensor(chip):
        for h in range(1, n_t):
            await_block(
                block(d, lax.rem(z - chip + n_z, n_z), lax.rem(t - h + n_t, n_t)),
                x_recv.at[h, chip],
            )
            to_core(h, chip)

    for i in order:
        await_block(block(d, lax.rem(z - i + n_z, n_z), t), z_recv.at[i])
        to_tensor(t, i)
        to_core(0, i)
    for i in [0] + order:
        from_tensor(i)
    for i in [0] + order:
        for h in range(n_t):
            for j in range(1, n_d):
                await_block(
                    block(
                        lax.rem(d - j + n_d, n_d),
                        lax.rem(z - i + n_z, n_z),
                        lax.rem(t - h + n_t, n_t),
                    ),
                    c_recv.at[j, h, i],
                )
    for copy in started:
        copy.wait_send()
    for i in range(blocks):
        for j in range(n_d):
            owner, core, copy = piece(i, j)
            if j:
                copy.wait_send()
            else:
                @pl.when(owner != t)
                def _():
                    copy.wait_send()


def experts_kernel(x, gate, up, weight, out):
    j = pl.program_id(0)
    lane = lax.broadcasted_iota(jnp.int32, weight.shape, 1)
    scale = jnp.sum(jnp.where(lane == j, weight[...], 0.0), axis=1, keepdims=True)
    g = jnp.dot(x[...], gate[0], preferred_element_type=jnp.float32)
    u = jnp.dot(x[...], up[0], preferred_element_type=jnp.float32)
    out[...] = (g / (1.0 + jnp.exp(-g)) * u * scale).astype(out.dtype)


def reduce_kernel(
    n_z, n_t, n_d, chunk, act, wd_hbm, out,
    wd, keep, core_out, core_in, half_out, half_in, own, chip_out, chip_in,
    wd_sem, c_send, c_recv, x_send, x_recv, z_send, z_recv,
):
    z, t, d = lax.axis_index("expert"), lax.axis_index("tensor"), lax.axis_index("dp")
    rows, width = out.shape
    per_half = width // chunk
    steps = n_t * per_half
    group = n_z * rows

    def half_of(s):
        return lax.rem(t + 1 + lax.rem(s, n_t), n_t)

    def load(s):
        column = pl.multiple_of(half_of(s) * width + (s // n_t) * chunk, chunk)
        return pltpu.make_async_copy(
            wd_hbm.at[:, pl.ds(column, chunk)], wd.at[s], wd_sem.at[s]
        )

    def core_copy(s):
        return pltpu.make_async_remote_copy(
            core_out.at[s], core_in.at[s], c_send.at[s], c_recv.at[s],
            device_id={"dp": 1 - d}, device_id_type=MESH,
        )

    def half_copy(s):
        h = lax.rem(s, n_t) + 1
        k = s // n_t
        return pltpu.make_async_remote_copy(
            half_out.at[h - 1, k], half_in.at[h - 1, k], x_send.at[h, k], x_recv.at[h, k],
            device_id={"tensor": lax.rem(t + h, n_t)}, device_id_type=MESH,
        )

    def chip_copy(i, k):
        target = lax.rem(z + i, n_z)
        return pltpu.make_async_remote_copy(
            chip_out.at[k, pl.ds(pl.multiple_of(target * rows, rows), rows)],
            chip_in.at[i, k], z_send.at[i, k], z_recv.at[i, k],
            device_id={"expert": target}, device_id_type=MESH,
        )

    for s in range(steps):
        load(s).start()
    greet(z, t, d, n_z, n_t, n_d, False)

    def core_arrival(s):
        core_copy(s).wait_recv()
        total = keep[lax.rem(s, 2)] + core_in[s].astype(jnp.float32)
        k = s // n_t

        @pl.when(lax.rem(s, n_t) != n_t - 1)
        def _():
            half_out[lax.rem(s, n_t), k] = total.astype(jnp.bfloat16)
            half_copy(s).start()

        @pl.when(lax.rem(s, n_t) == n_t - 1)
        def _():
            own[k] = total

    @pl.loop(0, steps)
    def _(s):
        load(s).wait()
        core_out[s] = jnp.dot(
            act[pl.ds(pl.multiple_of((1 - d) * group, group), group), :], wd[s],
            preferred_element_type=jnp.float32,
        ).astype(jnp.bfloat16)
        core_copy(s).start()
        keep[lax.rem(s, 2)] = jnp.dot(
            act[pl.ds(pl.multiple_of(d * group, group), group), :], wd[s],
            preferred_element_type=jnp.float32,
        )

        @pl.when(s > 0)
        def _():
            core_arrival(s - 1)

    core_arrival(steps - 1)

    @pl.loop(0, per_half)
    def _(k):
        total = own[k]
        for h in range(1, n_t):
            half_copy(k * n_t + h - 1).wait_recv()
            total = total + half_in[h - 1, k].astype(jnp.float32)
        own[k] = total
        chip_out[k] = total.astype(jnp.bfloat16)
        for i in range(1, n_z):
            chip_copy(i, k).start()

    @pl.loop(0, per_half)
    def _(k):
        total = own[k, pl.ds(pl.multiple_of(z * rows, rows), rows), :]
        for i in range(1, n_z):
            chip_copy(i, k).wait_recv()
            total = total + chip_in[i, k].astype(jnp.float32)
        out[:, pl.ds(pl.multiple_of(k * chunk, chunk), chunk)] = total.astype(out.dtype)

    @pl.loop(0, steps)
    def _(s):
        core_copy(s).wait_send()

        @pl.when(lax.rem(s, n_t) != n_t - 1)
        def _():
            half_copy(s).wait_send()

    @pl.loop(0, per_half)
    def _(k):
        for i in range(1, n_z):
            chip_copy(i, k).wait_send()


def on_device(
    attn, o_weight, residual, norm_gain, expert_ids, route_weights, w_gate, w_up, w_down
):
    n_z, n_t, n_d = lax.axis_size("expert"), lax.axis_size("tensor"), lax.axis_size("dp")
    z, d = lax.axis_index("expert"), lax.axis_index("dp")
    rows, depth = attn.shape
    width = residual.shape[1]
    full = norm_gain.shape[0]
    mine, _, hidden_units = w_gate.shape
    experts = mine * n_z * n_d
    all_rows = rows * n_z * n_d
    held = o_weight.shape[1]
    dma, vmem, bf16, f32 = pltpu.SemaphoreType.DMA, pltpu.VMEM, jnp.bfloat16, jnp.float32
    in_vmem = pl.BlockSpec(memory_space=pltpu.VMEM)
    in_any = pl.BlockSpec(memory_space=pl.ANY)

    named = expert_ids[:, :, None] == jnp.arange(experts, dtype=jnp.int32)
    weight_map = jnp.sum(jnp.where(named, route_weights[:, :, None], 0.0), axis=1)
    weight_map = lax.all_gather(weight_map, ("expert", "dp"), axis=0, tiled=True)
    weight_map = weight_map.reshape(n_z, n_d, rows, experts).transpose(1, 0, 2, 3)
    weight_map = lax.dynamic_slice_in_dim(
        weight_map.reshape(all_rows, experts), (z * n_d + d) * mine, mine, 1
    )

    x = pl.pallas_call(
        functools.partial(gather_kernel, n_z, n_t, n_d),
        out_shape=jax.ShapeDtypeStruct((all_rows, full), bf16),
        in_specs=[in_vmem, in_any, in_vmem, in_vmem],
        out_specs=in_vmem,
        scratch_shapes=[
            vmem((n_d * rows, depth), bf16),
            vmem((depth, held), bf16),
            vmem((n_d * rows, held), bf16),
            vmem((n_t, rows, width), bf16),
            vmem((n_t, rows, 128), f32),
            dma,
            dma((n_d,)), dma((n_d,)),
            dma((held // width, n_d)), dma((n_t,)),
            dma((n_t,)), dma((n_t,)),
            dma((n_z,)), dma((n_z,)),
            dma((n_t, n_z)), dma((n_t, n_z)),
            dma((n_d, n_t, n_z)), dma((n_d, n_t, n_z)),
        ],
        compiler_params=pltpu.CompilerParams(
            collective_id=0, has_side_effects=True, vmem_limit_bytes=40 * MIB
        ),
        name="project_gather",
    )(attn, o_weight, residual, norm_gain.reshape(1, full))

    tile = min(256, hidden_units)
    tiles = hidden_units // tile
    act = pl.pallas_call(
        experts_kernel,
        grid=(mine, tiles),
        out_shape=jax.ShapeDtypeStruct((all_rows, mine * hidden_units), bf16),
        in_specs=[
            pl.BlockSpec((all_rows, full), lambda j, i: (0, 0)),
            pl.BlockSpec((1, full, tile), lambda j, i: (j, 0, i)),
            pl.BlockSpec((1, full, tile), lambda j, i: (j, 0, i)),
            pl.BlockSpec((all_rows, mine), lambda j, i: (0, 0)),
        ],
        out_specs=pl.BlockSpec((all_rows, tile), lambda j, i: (0, j * tiles + i)),
        compiler_params=pltpu.CompilerParams(vmem_limit_bytes=56 * MIB),
        name="gate_up",
    )(x, w_gate, w_up, weight_map)

    chunk = min(512, width)
    per_half = width // chunk
    steps = n_t * per_half
    group = n_z * rows
    return pl.pallas_call(
        functools.partial(reduce_kernel, n_z, n_t, n_d, chunk),
        out_shape=jax.ShapeDtypeStruct((rows, width), bf16),
        in_specs=[in_vmem, in_any],
        out_specs=in_vmem,
        scratch_shapes=[
            vmem((steps, mine * hidden_units, chunk), bf16),
            vmem((2, group, chunk), f32),
            vmem((steps, group, chunk), bf16),
            vmem((steps, group, chunk), bf16),
            vmem((n_t - 1, per_half, group, chunk), bf16),
            vmem((n_t - 1, per_half, group, chunk), bf16),
            vmem((per_half, group, chunk), f32),
            vmem((per_half, group, chunk), bf16),
            vmem((n_z, per_half, rows, chunk), bf16),
            dma((steps,)),
            dma((steps,)), dma((steps,)),
            dma((n_t, per_half)), dma((n_t, per_half)),
            dma((n_z, per_half)), dma((n_z, per_half)),
        ],
        compiler_params=pltpu.CompilerParams(
            collective_id=1, has_side_effects=True, vmem_limit_bytes=56 * MIB
        ),
        name="down_reduce",
    )(act, w_down.reshape(mine * hidden_units, full))


def solution(mesh):
    rows = ("groups", "expert", "dp")
    return jax.shard_map(
        on_device,
        mesh=mesh,
        in_specs=(
            P(rows, "tensor"),
            P("tensor", "dp"),
            P(rows, "tensor"),
            P(),
            P(rows, None),
            P(rows, None),
            P(("expert", "dp"), None, "tensor"),
            P(("expert", "dp"), None, "tensor"),
            P(("expert", "dp"), "tensor", None),
        ),
        out_specs=P(rows, "tensor"),
        check_vma=False,
    )
```

time: 422 us -> 142 us (0.34)
  blocking collectives: 219 us -> 15.7 us
  waiting for transfers between devices: 140 us -> 0 us
  Pallas kernels: 0 us -> 114 us
  matrix products: 44.9 us -> 0 us
  between operations: 13.2 us -> 0.04 us
  local copies, waits for them, and re-layouts: 2.36 us -> 10.6 us
    all_to_all x2 -> x0, blocking collectives: 219 us -> none  [the longest x1 144 us: on_device(): lax.all_to_all(outgoing, ('expert', 'dp'), split_axis=0, concat_axis=0, t...]
    pallas_call x0 -> x3, Pallas kernels: none -> 114 us  [the longest x1 49.8 us: on_device(): pl.pallas_call(functools.partial(gather_kernel, n_z, n_t, n_d), out_shape...]
    reduce_scatter x1 -> x0, waiting for transfers between devices: 75 us -> none  [on_device(): lax.psum_scatter(partials.astype(jnp.bfloat16), 'tensor', scatter_dimensi...]
    dot_general x7 -> x0, matrix products: 44.9 us -> none  [the longest x1 11.9 us: on_device(): jnp.einsum('sjcf,jfd->sjcd', activated, w_down, preferred_element_type=jn...]
    all_gather x1 -> x0, waiting for transfers between devices: 34.3 us -> none  [on_device(): lax.all_gather(o_weight, 'dp', axis=1, tiled=True)]
    psum x1 -> x0, waiting for transfers between devices: 29.6 us -> none  [on_device(): summed = lax.psum(partial_value.astype(jnp.bfloat16), 'tensor')]
    all_gather x0 -> x1, blocking collectives: none -> 15.7 us  [on_device(): lax.all_gather(weight_map, ('expert', 'dp'), axis=0, tiled=True)]
    unnamed x12 -> x9, local copies, waits for them, and re-layouts: 0.03 us -> 8.88 us
  transfers between devices with their start and end apart: 3 -> 0, of which waited for: 3 -> 0; matrix products, arithmetic and copies ran while one was open for 0% -> 0% of each run, Pallas kernels for 0% -> 0%
where the time goes in v1:
time: 142 us; the launch traced here: 141 us
  Pallas kernels  114 us (80%)
  blocking collectives  15.7 us (11%)
  local copies, waits for them, and re-layouts  10.6 us (7%)
    pallas_call x1, Pallas kernels, on_device(): pl.pallas_call(functools.partial(gather_kernel, n_z, n_t, n_d), out_shape...  49.8 us
    pallas_call x1, Pallas kernels, on_device(): pl.pallas_call(functools.partial(reduce_kernel, n_z, n_t, n_d, chunk), ou...  41.3 us
    pallas_call x1, Pallas kernels, on_device(): pl.pallas_call(experts_kernel, grid=(mine, tiles), out_shape=jax.ShapeDty...  23.3 us
    all_gather x1, blocking collectives, on_device(): lax.all_gather(weight_map, ('expert', 'dp'), axis=0, tiled=True)  15.7 us
    unnamed x9, local copies, waits for them, and re-layouts  8.88 us

profile of v1, /device:TPU:0, one launch (start us, length us, event | category | flops | bytes accessed | tf_op | source)
XLA Modules:
  0.0 141.5 jit_solution(7501529162283507776)
XLA Ops:
  0.0 0.7 reshape.14.gain
  0.7 0.7 select_reduce_fusion
  1.4 15.7 %all-gather = f32[8,64,32]{1,2,0:T(8,128)S(1)} all-gather(f32[1,64,32]{1,2,0:T(8,128)S(1)} %bitcast.9), channel_id=1, replica_groups=mesh['groups'=2,'expert'=4,'tensor'=2,'dp'=2] {'expert','dp'}, dimensions={0}, use_global_device_ids=true | all-gather | bytes 73728 | tf_op jit(solution)/shard_map/all_gather | solution.py:353
  17.2 0.1 copy.18
  17.3 0.8 constant_dynamic-slice_fusion.weight
  18.1 0.0 copy-start.1
  18.1 3.4 %copy-done.1 = bf16[2048,2048]{1,0:T(8,128)(2,1)S(1)} copy-done((bf16[2048,2048]{1,0:T(8,128)(2,1)S(1)}, bf16[2048,2048]{1,0:T(8,128)(2,1)}, u32[]{:S(2)}) %copy-start.1) | copy-done | bytes 8388632
  21.5 0.0 copy-start.2
  21.5 0.9 copy-done.2
  22.5 0.0 copy-start.3
  22.5 0.9 copy-done.3
  23.4 49.8 %project_gather.1.x = bf16[512,4096]{1,0:T(8,128)(2,1)S(1)} custom-call(bf16[64,2048]{1,0:T(8,128)(2,1)S(1)} %copy-done.2, bf16[2048,2048]{1,0:T(8,128)(2,1)S(1)} %copy-done.1, bf16[64,2048]{1,0:T(8,128)(2,1)S(1)} %copy-done.3, bf16[1,4096]{1,0:T(2,128)(2,1)S(1)} %reshape.14.gain), custom_call_target="tpu_custom_call" | custom-call | tf_op jit(solution)/shard_map/project_gather/pallas_call | solution.py:359
  73.3 0.0 copy-start
  73.3 1.9 %copy-done = bf16[512,4096]{1,0:T(8,128)(2,1)} copy-done((bf16[512,4096]{1,0:T(8,128)(2,1)}, bf16[512,4096]{1,0:T(8,128)(2,1)S(1)}, u32[]{:S(2)}) %copy-start) | copy-done | bytes 4194328
  75.2 23.3 %gate_up.1.act = bf16[512,2048]{1,0:T(8,128)(2,1)} custom-call(bf16[512,4096]{1,0:T(8,128)(2,1)} %copy-done, bf16[4,4096,512]{2,1,0:T(8,128)(2,1)} %gate.1, bf16[4,4096,512]{2,1,0:T(8,128)(2,1)} %up.1, f32[512,4]{1,0:T(8,128)} %constant_dynamic-slice_fusion.weight), custom_call_target="tpu_custom_call" | custom-call | tf_op jit(solution)/shard_map/gate_up/pallas_call | solution.py:386
  98.5 41.3 %down_reduce.1 = bf16[64,2048]{1,0:T(8,128)(2,1)} custom-call(bf16[512,2048]{1,0:T(8,128)(2,1)} %gate_up.1.act, bf16[2048,4096]{1,0:T(8,128)(2,1)} %bitcast.6), custom_call_target="tpu_custom_call" | custom-call | tf_op jit(solution)/shard_map/down_reduce/pallas_call | solution.py:405
  139.8 1.7 %copy.20 = bf16[64,2048]{1,0:T(8,128)(2,1)} copy(bf16[64,2048]{1,0:T(8,128)(2,1)} %down_reduce.1) | data formatting | bytes 524288
Async XLA Ops:
  18.1 3.4 %copy-start.1 = (bf16[2048,2048]{1,0:T(8,128)(2,1)S(1)}, bf16[2048,2048]{1,0:T(8,128)(2,1)}, u32[]{:S(2)}) copy-start(bf16[2048,2048]{1,0:T(8,128)(2,1)} %ow_hbm.1) | copy-start | bytes 25165828
  21.5 0.9 copy-start.2
  22.5 0.9 copy-start.3
  73.3 1.9 %copy-start = (bf16[512,4096]{1,0:T(8,128)(2,1)}, bf16[512,4096]{1,0:T(8,128)(2,1)S(1)}, u32[]{:S(2)}) copy-start(bf16[512,4096]{1,0:T(8,128)(2,1)S(1)} %project_gather.1.x) | copy-start | bytes 12582916

commit v2 on v1

--- a/solution.py
+++ b/solution.py
@@ -34,29 +34,47 @@
 
 
 def gather_kernel(
-    n_z, n_t, n_d, attn, ow_hbm, residual, gain, out,
-    pair, ow, part, landed, squares,
-    ow_sem, a_send, a_recv, p_send, p_recv, s_send, s_recv,
+    n_z, n_t, n_d, attn_hbm, ow_hbm, residual_hbm, gain, routes, out, all_routes,
+    pair, residual, ow, part, landed, squares,
+    ow_sem, in_sem, m_send, m_recv, n_send, n_recv, a_send, a_recv, p_send, p_recv, s_send, s_recv,
     z_send, z_recv, x_send, x_recv, c_send, c_recv,
 ):
     z, t, d = lax.axis_index("expert"), lax.axis_index("tensor"), lax.axis_index("dp")
-    rows, depth = attn.shape
-    width = residual.shape[1]
+    rows, width = residual.shape
     held = ow.shape[1]
     blocks = held // width
+    attn = pair.at[pl.ds(pl.multiple_of(d * rows, rows), rows), :]
+    load_attn = pltpu.make_async_copy(attn_hbm, attn, in_sem.at[0])
+    load_attn.start()
+    load_residual = pltpu.make_async_copy(residual_hbm, residual, in_sem.at[1])
+    load_residual.start()
     load = pltpu.make_async_copy(ow_hbm, ow, ow_sem)
     load.start()
     greet(z, t, d, n_z, n_t, n_d, True)
 
-    pair[pl.ds(d * rows, rows), :] = attn[...]
+    load_attn.wait()
     sent = []
     for j in range(1, n_d):
         copy = pltpu.make_async_remote_copy(
-            attn, pair.at[pl.ds(d * rows, rows), :], a_send.at[j], a_recv.at[j],
+            attn, attn, a_send.at[j], a_recv.at[j],
             device_id={"dp": lax.rem(d + j, n_d)}, device_id_type=MESH,
         )
         copy.start()
         sent.append(copy)
+    def routes_of(core, chip):
+        first = pl.multiple_of((core * n_z + chip) * rows, rows)
+        return all_routes.at[pl.ds(first, rows), :]
+
+    routes_of(d, z)[...] = routes[...]
+    maps = []
+    for i in range(1, n_z):
+        copy = pltpu.make_async_remote_copy(
+            routes, routes_of(d, z), m_send.at[i], m_recv.at[i],
+            device_id={"expert": lax.rem(z + i, n_z)}, device_id_type=MESH,
+        )
+        copy.start()
+        maps.append(copy)
+
     load.wait()
     for copy in sent:
         copy.wait()
@@ -100,6 +118,7 @@
         def _():
             arrival.wait_recv()
 
+    load_residual.wait()
     hidden = residual[...].astype(jnp.float32)
     for i in range(n_t):
         hidden = hidden + landed[i].astype(jnp.float32)
@@ -167,6 +186,22 @@
         copy.start()
         started.append(copy)
     to_core(0, 0)
+    for i, copy in enumerate(maps):
+        copy.wait_send()
+        ref = routes_of(d, lax.rem(z - i - 1 + n_z, n_z))
+        pltpu.make_async_remote_copy(
+            ref, ref, m_send.at[i + 1], m_recv.at[i + 1],
+            device_id={"tensor": t}, device_id_type=MESH,
+        ).wait_recv()
+    turned = []
+    for j in range(1, n_d):
+        ref = all_routes.at[pl.ds(pl.multiple_of(d * n_z * rows, rows), n_z * rows), :]
+        copy = pltpu.make_async_remote_copy(
+            ref, ref, n_send.at[j], n_recv.at[j],
+            device_id={"dp": lax.rem(d + j, n_d)}, device_id_type=MESH,
+        )
+        copy.start()
+        turned.append(copy)
 
     def await_block(ref, sem):
         pltpu.make_async_remote_copy(
@@ -198,6 +233,8 @@
                     ),
                     c_recv.at[j, h, i],
                 )
+    for copy in turned:
+        copy.wait()
     for copy in started:
         copy.wait_send()
     for i in range(blocks):
@@ -211,10 +248,11 @@
                     copy.wait_send()
 
 
-def experts_kernel(x, gate, up, weight, out):
+def experts_kernel(n_d, mine, x, gate, up, weight, out):
     j = pl.program_id(0)
+    first = (lax.axis_index("expert") * n_d + lax.axis_index("dp")) * mine
     lane = lax.broadcasted_iota(jnp.int32, weight.shape, 1)
-    scale = jnp.sum(jnp.where(lane == j, weight[...], 0.0), axis=1, keepdims=True)
+    scale = jnp.sum(jnp.where(lane == first + j, weight[...], 0.0), axis=1, keepdims=True)
     g = jnp.dot(x[...], gate[0], preferred_element_type=jnp.float32)
     u = jnp.dot(x[...], up[0], preferred_element_type=jnp.float32)
     out[...] = (g / (1.0 + jnp.exp(-g)) * u * scale).astype(out.dtype)
@@ -336,7 +374,6 @@
     attn, o_weight, residual, norm_gain, expert_ids, route_weights, w_gate, w_up, w_down
 ):
     n_z, n_t, n_d = lax.axis_size("expert"), lax.axis_size("tensor"), lax.axis_size("dp")
-    z, d = lax.axis_index("expert"), lax.axis_index("dp")
     rows, depth = attn.shape
     width = residual.shape[1]
     full = norm_gain.shape[0]
@@ -350,24 +387,26 @@
 
     named = expert_ids[:, :, None] == jnp.arange(experts, dtype=jnp.int32)
     weight_map = jnp.sum(jnp.where(named, route_weights[:, :, None], 0.0), axis=1)
-    weight_map = lax.all_gather(weight_map, ("expert", "dp"), axis=0, tiled=True)
-    weight_map = weight_map.reshape(n_z, n_d, rows, experts).transpose(1, 0, 2, 3)
-    weight_map = lax.dynamic_slice_in_dim(
-        weight_map.reshape(all_rows, experts), (z * n_d + d) * mine, mine, 1
-    )
-
-    x = pl.pallas_call(
+    lanes = -(-experts // 128) * 128
+    weight_map = jnp.pad(weight_map, ((0, 0), (0, lanes - experts)))
+
+    x, weight_map = pl.pallas_call(
         functools.partial(gather_kernel, n_z, n_t, n_d),
-        out_shape=jax.ShapeDtypeStruct((all_rows, full), bf16),
-        in_specs=[in_vmem, in_any, in_vmem, in_vmem],
-        out_specs=in_vmem,
+        out_shape=[
+            jax.ShapeDtypeStruct((all_rows, full), bf16),
+            jax.ShapeDtypeStruct((all_rows, lanes), f32),
+        ],
+        in_specs=[in_any, in_any, in_any, in_vmem, in_vmem],
+        out_specs=[in_vmem, in_vmem],
         scratch_shapes=[
             vmem((n_d * rows, depth), bf16),
+            vmem((rows, width), bf16),
             vmem((depth, held), bf16),
             vmem((n_d * rows, held), bf16),
             vmem((n_t, rows, width), bf16),
             vmem((n_t, rows, 128), f32),
-            dma,
+            dma, dma((2,)),
+            dma((n_z,)), dma((n_z,)), dma((n_d,)), dma((n_d,)),
             dma((n_d,)), dma((n_d,)),
             dma((held // width, n_d)), dma((n_t,)),
             dma((n_t,)), dma((n_t,)),
@@ -376,22 +415,22 @@
             dma((n_d, n_t, n_z)), dma((n_d, n_t, n_z)),
         ],
         compiler_params=pltpu.CompilerParams(
-            collective_id=0, has_side_effects=True, vmem_limit_bytes=40 * MIB
+            collective_id=0, has_side_effects=True, vmem_limit_bytes=60 * MIB
         ),
         name="project_gather",
-    )(attn, o_weight, residual, norm_gain.reshape(1, full))
+    )(attn, o_weight, residual, norm_gain.reshape(1, full), weight_map)
 
     tile = min(256, hidden_units)
     tiles = hidden_units // tile
     act = pl.pallas_call(
-        experts_kernel,
+        functools.partial(experts_kernel, n_d, mine),
         grid=(mine, tiles),
         out_shape=jax.ShapeDtypeStruct((all_rows, mine * hidden_units), bf16),
         in_specs=[
             pl.BlockSpec((all_rows, full), lambda j, i: (0, 0)),
             pl.BlockSpec((1, full, tile), lambda j, i: (j, 0, i)),
             pl.BlockSpec((1, full, tile), lambda j, i: (j, 0, i)),
-            pl.BlockSpec((all_rows, mine), lambda j, i: (0, 0)),
+            pl.BlockSpec((all_rows, lanes), lambda j, i: (0, 0)),
         ],
         out_specs=pl.BlockSpec((all_rows, tile), lambda j, i: (0, j * tiles + i)),
         compiler_params=pltpu.CompilerParams(vmem_limit_bytes=56 * MIB),

time: 142 us -> 125 us (0.88)
  blocking collectives: 15.7 us -> 0 us
  local copies, waits for them, and re-layouts: 10.6 us -> 3.68 us
  Pallas kernels: 114 us -> 120 us
    all_gather x1 -> x0, blocking collectives: 15.7 us -> none  [on_device(): lax.all_gather(weight_map, ('expert', 'dp'), axis=0, tiled=True)]
    unnamed x9 -> x1, local copies, waits for them, and re-layouts: 8.88 us -> 1.67 us
    pallas_call x1, Pallas kernels: 49.8 us -> 55.6 us  [on_device(): pl.pallas_call(functools.partial(gather_kernel, n_z, n_t, n_d), out_shape...]
where the time goes in v2:
time: 125 us
  Pallas kernels  120 us (96%)
  local copies, waits for them, and re-layouts  3.68 us (3%)
    pallas_call x1, Pallas kernels, on_device(): pl.pallas_call(functools.partial(gather_kernel, n_z, n_t, n_d), out_shape...  55.6 us
    pallas_call x1, Pallas kernels, on_device(): pl.pallas_call(functools.partial(reduce_kernel, n_z, n_t, n_d, chunk), ou...  41.3 us
    pallas_call x1, Pallas kernels, on_device(): pl.pallas_call(functools.partial(experts_kernel, n_d, mine), grid=(mine,...  23.4 us

profile of v2, /device:TPU:0, one launch (start us, length us, event | category | flops | bytes accessed | tf_op | source)
XLA Modules:
  0.0 124.7 jit_solution(2656998141928265769)
XLA Ops:
  0.0 1.3 %reshape.8.gain = bf16[1,4096]{1,0:T(2,128)(2,1)} reshape(bf16[4096]{0:T(1024)(128)(2,1)} %param.12) | data formatting | bytes 16384 | tf_op jit(solution)/shard_map/reshape | solution.py:421
  1.3 0.7 select_reduce_fusion
  2.0 0.1 copy.12
  2.1 0.6 pad.4.routes
  2.7 55.6 %project_gather.1 = (bf16[512,4096]{1,0:T(8,128)(2,1)}, f32[512,128]{1,0:T(8,128)}) custom-call(bf16[64,2048]{1,0:T(8,128)(2,1)} %attn_hbm.1, bf16[2048,2048]{1,0:T(8,128)(2,1)} %ow_hbm.1, bf16[64,2048]{1,0:T(8,128)(2,1)} %residual_hbm.1, bf16[1,4096]{1,0:T(2,128)(2,1)} %reshape.8.gain, f32[64,128]{1,0:T(8,128)} %pad.4.routes), custom_call_target="tpu_custom_call" | custom-call | tf_op jit(solution)/shard_map/project_gather/pallas_call | solution.py:393
  58.4 23.4 %gate_up.1.act = bf16[512,2048]{1,0:T(8,128)(2,1)} custom-call(bf16[512,4096]{1,0:T(8,128)(2,1)} %get-tuple-element.7.x, bf16[4,4096,512]{2,1,0:T(8,128)(2,1)} %gate.1, bf16[4,4096,512]{2,1,0:T(8,128)(2,1)} %up.1, f32[512,128]{1,0:T(8,128)} %get-tuple-element.8.weight), custom_call_target="tpu_custom_call" | custom-call | tf_op jit(solution)/shard_map/gate_up/pallas_call | solution.py:425
  81.7 41.3 %down_reduce.1 = bf16[64,2048]{1,0:T(8,128)(2,1)} custom-call(bf16[512,2048]{1,0:T(8,128)(2,1)} %gate_up.1.act, bf16[2048,4096]{1,0:T(8,128)(2,1)} %bitcast.1), custom_call_target="tpu_custom_call" | custom-call | tf_op jit(solution)/shard_map/down_reduce/pallas_call | solution.py:444
  123.0 1.7 %copy.14 = bf16[64,2048]{1,0:T(8,128)(2,1)} copy(bf16[64,2048]{1,0:T(8,128)(2,1)} %down_reduce.1) | data formatting | bytes 524288

commit v3 on v2

--- a/solution.py
+++ b/solution.py
@@ -34,8 +34,8 @@
 
 
 def gather_kernel(
-    n_z, n_t, n_d, attn_hbm, ow_hbm, residual_hbm, gain, routes, out, all_routes,
-    pair, residual, ow, part, landed, squares,
+    n_z, n_t, n_d, attn_hbm, ow_hbm, residual_hbm, gain, routes, gate_hbm, up_hbm, act,
+    out, all_routes, tiles, sums_of, tile_sem, pair, residual, ow, part, landed, squares,
     ow_sem, in_sem, m_send, m_recv, n_send, n_recv, a_send, a_recv, p_send, p_recv, s_send, s_recv,
     z_send, z_recv, x_send, x_recv, c_send, c_recv,
 ):
@@ -50,6 +50,18 @@
     load_residual.start()
     load = pltpu.make_async_copy(ow_hbm, ow, ow_sem)
     load.start()
+    mine, _, units = gate_hbm.shape
+    slots = tiles.shape[0]
+    count = 2 * mine * n_t
+
+    def load_tile(n):
+        h, j = n // (2 * mine), n % (2 * mine) // 2
+        first = pl.multiple_of(lax.rem(t - h + n_t, n_t) * width, width)
+        source = (up_hbm if n % 2 else gate_hbm).at[j, pl.ds(first, width), :]
+        return pltpu.make_async_copy(source, tiles.at[n % slots], tile_sem.at[n % slots])
+
+    for n in range(min(slots, count)):
+        load_tile(n).start()
     greet(z, t, d, n_z, n_t, n_d, True)
 
     load_attn.wait()
@@ -220,10 +232,8 @@
         await_block(block(d, lax.rem(z - i + n_z, n_z), t), z_recv.at[i])
         to_tensor(t, i)
         to_core(0, i)
-    for i in [0] + order:
-        from_tensor(i)
-    for i in [0] + order:
-        for h in range(n_t):
+    def await_core(h):
+        for i in [0] + order:
             for j in range(1, n_d):
                 await_block(
                     block(
@@ -233,8 +243,54 @@
                     ),
                     c_recv.at[j, h, i],
                 )
+
+    step = min(256, units)
+    lane = lax.broadcasted_iota(jnp.int32, all_routes.shape, 1)
+    base = (z * n_d + d) * mine
+
+    def product(h, j):
+        n = (h * mine + j) * 2
+        load_tile(n).wait()
+        load_tile(n + 1).wait()
+        features = out.at[:, pl.ds(pl.multiple_of(lax.rem(t - h + n_t, n_t) * width, width), width)]
+        if h == n_t - 1:
+            scale = jnp.sum(jnp.where(lane == base + j, all_routes[...], 0.0), axis=1, keepdims=True)
+        for first in range(0, units, step):
+            cols = pl.ds(first, step)
+            both = []
+            for side in range(2):
+                value = jnp.dot(
+                    features[...], tiles[(n + side) % slots, :, cols],
+                    preferred_element_type=jnp.float32,
+                )
+                if h:
+                    value = value + sums_of[2 * j + side, :, cols]
+                if h < n_t - 1:
+                    sums_of[2 * j + side, :, cols] = value
+                both.append(value)
+            if h == n_t - 1:
+                g, u = both
+                act[:, pl.ds(j * units + first, step)] = (
+                    g / (1.0 + jnp.exp(-g)) * u * scale
+                ).astype(act.dtype)
+        for later in (n + slots, n + 1 + slots):
+            if later < count:
+                load_tile(later).start()
+
+    chips = [0] + order
+    from_tensor(chips.pop(0))
+    await_core(0)
     for copy in turned:
         copy.wait()
+    for h in range(n_t):
+        if h:
+            await_core(h)
+        for j in range(mine):
+            product(h, j)
+            if h == 0 and j < mine - 1 and chips:
+                from_tensor(chips.pop(0))
+        while chips:
+            from_tensor(chips.pop(0))
     for copy in started:
         copy.wait_send()
     for i in range(blocks):
@@ -246,16 +302,6 @@
                 @pl.when(owner != t)
                 def _():
                     copy.wait_send()
-
-
-def experts_kernel(n_d, mine, x, gate, up, weight, out):
-    j = pl.program_id(0)
-    first = (lax.axis_index("expert") * n_d + lax.axis_index("dp")) * mine
-    lane = lax.broadcasted_iota(jnp.int32, weight.shape, 1)
-    scale = jnp.sum(jnp.where(lane == first + j, weight[...], 0.0), axis=1, keepdims=True)
-    g = jnp.dot(x[...], gate[0], preferred_element_type=jnp.float32)
-    u = jnp.dot(x[...], up[0], preferred_element_type=jnp.float32)
-    out[...] = (g / (1.0 + jnp.exp(-g)) * u * scale).astype(out.dtype)
 
 
 def reduce_kernel(
@@ -390,15 +436,17 @@
     lanes = -(-experts // 128) * 128
     weight_map = jnp.pad(weight_map, ((0, 0), (0, lanes - experts)))
 
-    x, weight_map = pl.pallas_call(
+    act = pl.pallas_call(
         functools.partial(gather_kernel, n_z, n_t, n_d),
-        out_shape=[
-            jax.ShapeDtypeStruct((all_rows, full), bf16),
-            jax.ShapeDtypeStruct((all_rows, lanes), f32),
-        ],
-        in_specs=[in_any, in_any, in_any, in_vmem, in_vmem],
-        out_specs=[in_vmem, in_vmem],
+        out_shape=jax.ShapeDtypeStruct((all_rows, mine * hidden_units), bf16),
+        in_specs=[in_any, in_any, in_any, in_vmem, in_vmem, in_any, in_any],
+        out_specs=in_vmem,
         scratch_shapes=[
+            vmem((all_rows, full), bf16),
+            vmem((all_rows, lanes), f32),
+            vmem((2 * mine, width, hidden_units), bf16),
+            vmem((2 * mine, all_rows, hidden_units), f32),
+            dma((2 * mine,)),
             vmem((n_d * rows, depth), bf16),
             vmem((rows, width), bf16),
             vmem((depth, held), bf16),
@@ -417,25 +465,8 @@
         compiler_params=pltpu.CompilerParams(
             collective_id=0, has_side_effects=True, vmem_limit_bytes=60 * MIB
         ),
-        name="project_gather",
-    )(attn, o_weight, residual, norm_gain.reshape(1, full), weight_map)
-
-    tile = min(256, hidden_units)
-    tiles = hidden_units // tile
-    act = pl.pallas_call(
-        functools.partial(experts_kernel, n_d, mine),
-        grid=(mine, tiles),
-        out_shape=jax.ShapeDtypeStruct((all_rows, mine * hidden_units), bf16),
-        in_specs=[
-            pl.BlockSpec((all_rows, full), lambda j, i: (0, 0)),
-            pl.BlockSpec((1, full, tile), lambda j, i: (j, 0, i)),
-            pl.BlockSpec((1, full, tile), lambda j, i: (j, 0, i)),
-            pl.BlockSpec((all_rows, lanes), lambda j, i: (0, 0)),
-        ],
-        out_specs=pl.BlockSpec((all_rows, tile), lambda j, i: (0, j * tiles + i)),
-        compiler_params=pltpu.CompilerParams(vmem_limit_bytes=56 * MIB),
-        name="gate_up",
-    )(x, w_gate, w_up, weight_map)
+        name="project_gather_gate_up",
+    )(attn, o_weight, residual, norm_gain.reshape(1, full), weight_map, w_gate, w_up)
 
     chunk = min(512, width)
     per_half = width // chunk

time: 125 us -> 115 us (0.920)
  Pallas kernels: 120 us -> 111 us
    pallas_call x1 -> x0, Pallas kernels: 23.4 us -> none  [on_device(): pl.pallas_call(functools.partial(experts_kernel, n_d, mine), grid=(mine,...]
    pallas_call x1, Pallas kernels: 55.6 us -> 68.8 us  [on_device(): pl.pallas_call(functools.partial(gather_kernel, n_z, n_t, n_d), out_shape...]
where the time goes in v3:
time: 115 us
  Pallas kernels  111 us (97%)
  local copies, waits for them, and re-layouts  3.68 us (3%)
    pallas_call x1, Pallas kernels, on_device(): pl.pallas_call(functools.partial(gather_kernel, n_z, n_t, n_d), out_shape...  68.8 us
    pallas_call x1, Pallas kernels, on_device(): pl.pallas_call(functools.partial(reduce_kernel, n_z, n_t, n_d, chunk), ou...  41.8 us

profile of v3, /device:TPU:0, one launch (start us, length us, event | category | flops | bytes accessed | tf_op | source)
XLA Modules:
  0.0 115.0 jit_solution(6436209394419199945)
XLA Ops:
  0.0 1.3 %reshape.8.gain = bf16[1,4096]{1,0:T(2,128)(2,1)} reshape(bf16[4096]{0:T(1024)(128)(2,1)} %param.12) | data formatting | bytes 16384 | tf_op jit(solution)/shard_map/reshape | solution.py:469
  1.3 0.7 select_reduce_fusion
  2.0 0.1 copy.12
  2.1 0.6 pad.4.routes
  2.7 68.8 %project_gather_gate_up.1.act = bf16[512,2048]{1,0:T(8,128)(2,1)} custom-call(bf16[64,2048]{1,0:T(8,128)(2,1)} %attn_hbm.1, bf16[2048,2048]{1,0:T(8,128)(2,1)} %ow_hbm.1, bf16[64,2048]{1,0:T(8,128)(2,1)} %residual_hbm.1, bf16[1,4096]{1,0:T(2,128)(2,1)} %reshape.8.gain, f32[64,128]{1,0:T(8,128)} %pad.4.routes, bf16[4,4096,512]{2,1,0:T(8,128)(2,1)} %gate_hbm.1, ...), custom_call_target="tpu_custom_call" | custom-call | tf_op jit(solution)/shard_map/project_gather_gate_up/pallas_call | solution.py:439
  71.6 41.8 %down_reduce.1 = bf16[64,2048]{1,0:T(8,128)(2,1)} custom-call(bf16[512,2048]{1,0:T(8,128)(2,1)} %project_gather_gate_up.1.act, bf16[2048,4096]{1,0:T(8,128)(2,1)} %bitcast.1), custom_call_target="tpu_custom_call" | custom-call | tf_op jit(solution)/shard_map/down_reduce/pallas_call | solution.py:475
  113.3 1.7 %copy.14 = bf16[64,2048]{1,0:T(8,128)(2,1)} copy(bf16[64,2048]{1,0:T(8,128)(2,1)} %down_reduce.1) | data formatting | bytes 524288
